TPU v7x, 32 devices: a whole 2x2x4 slice. The times are simulated.
32 devices in a mesh: row: 4 (over z), col: 8 (over y, x, core).
Axes of the slice: x: 2, y: 2, z: 4, core: 2. Of those that a mesh axis runs over, the one named last changes fastest.
Arguments:
- inputs: bfloat16 [256, 8192], P('col', 'row'), may hold values from -6 to 6
- out_grad: bfloat16 [256, 8192], P('col', 'row'), may hold values from -6 to 6
- w_gate: bfloat16 [8192, 16384], P('row', 'col'), may hold values from -0.0625 to 0.0625
- w_up: bfloat16 [8192, 16384], P('row', 'col'), may hold values from -0.0625 to 0.0625
- w_down: bfloat16 [16384, 8192], P('col', 'row'), may hold values from -0.046875 to 0.046875
Outputs:
- input_grad: bfloat16 [256, 8192], P('col', 'row')
- gate_wgrad: bfloat16 [8192, 16384], P('row', 'col')
- up_wgrad: bfloat16 [8192, 16384], P('row', 'col')
- down_wgrad: bfloat16 [16384, 8192], P('col', 'row')
All inputs are finite; a program needn't handle non-finite values.
Results may differ from a plain program's by a relative error of at most 0.02.
Values may be sent and summed in bfloat16 or wider, within the bound.
A program may use at most 128 MiB of HBM per device.

v0:
```python
import jax
import jax.numpy as jnp
from jax import lax
from jax.sharding import PartitionSpec as P


def swiglu_back(summed, width):
    gate = summed[:, :width]
    up = summed[:, width : 2 * width]
    hidden_grad = summed[:, 2 * width :]
    sig = jax.nn.sigmoid(gate)
    act = gate * sig
    hidden = (act * up).astype(jnp.bfloat16)
    up_delta = (hidden_grad * act).astype(jnp.bfloat16)
    gate_delta = (hidden_grad * up * sig * (1.0 + gate * (1.0 - sig))).astype(jnp.bfloat16)
    return (hidden, gate_delta, up_delta)


def on_device(inputs, out_grad, w_gate, w_up, w_down):
    inputs_all, cotan_all = (
        lax.all_gather(inputs, "col", axis=0, tiled=True),
        lax.all_gather(out_grad, "col", axis=0, tiled=True),
    )
    width = w_gate.shape[1]
    rest = (((1,), (1,)), ((), ()))
    gate = jnp.dot(inputs_all, w_gate, preferred_element_type=jnp.float32)
    up = jnp.dot(inputs_all, w_up, preferred_element_type=jnp.float32)
    back = lax.dot_general(cotan_all, w_down, rest, preferred_element_type=jnp.float32)
    summed = lax.psum_scatter(
        jnp.concatenate([gate, up, back], axis=1).astype(jnp.bfloat16),
        "row",
        scatter_dimension=0,
        tiled=True,
    ).astype(jnp.float32)
    hidden, gate_delta, up_delta = swiglu_back(summed, width)
    hidden_all, gate_all, up_all = (
        lax.all_gather(hidden, "row", axis=0, tiled=True),
        lax.all_gather(gate_delta, "row", axis=0, tiled=True),
        lax.all_gather(up_delta, "row", axis=0, tiled=True),
    )
    first = lax.dot_general(gate_all, w_gate, rest, preferred_element_type=jnp.float32)
    input_grad = lax.psum_scatter(
        (first + lax.dot_general(up_all, w_up, rest, preferred_element_type=jnp.float32)).astype(
            jnp.bfloat16
        ),
        "col",
        scatter_dimension=0,
        tiled=True,
    )
    contract = (((0,), (0,)), ((), ()))
    gate_wgrad = lax.dot_general(
        inputs_all, gate_all, contract, preferred_element_type=jnp.float32
    ).astype(jnp.bfloat16)
    up_wgrad = lax.dot_general(
        inputs_all, up_all, contract, preferred_element_type=jnp.float32
    ).astype(jnp.bfloat16)
    down_wgrad = lax.dot_general(
        hidden_all, cotan_all, contract, preferred_element_type=jnp.float32
    ).astype(jnp.bfloat16)
    return (input_grad, gate_wgrad, up_wgrad, down_wgrad)


def solution(mesh):
    in_specs = (P("col", "row"), P("col", "row"), P("row", "col"), P("row", "col"), P("col", "row"))
    out_specs = (P("col", "row"), P("row", "col"), P("row", "col"), P("col", "row"))
    return jax.shard_map(
        on_device, mesh=mesh, in_specs=in_specs, out_specs=out_specs, check_vma=False
    )
```

profile of v0, /device:TPU:0, one launch (start us, length us, event | category | flops | bytes accessed | tf_op | source)
XLA Modules:
  0.0 264.8 jit_solution(1818214111084297650)
XLA Ops:
  7.2 0.0 all-gather.6.cloned.1.call-start
  7.2 0.7 all-gather.6.cloned.1.call-update
  7.9 0.0 all-gather.8.cloned.1.call-start
  7.9 0.7 all-gather.8.cloned.1.call-update
  8.6 0.0 reduce-scatter.3.cloned.1.call-start
  8.7 27.4 %all-gather.6.cloned.1.call-done = bf16[256,2048]{1,0:T(8,128)(2,1)} async-done(((bf16[32,2048]{1,0:T(8,128)(2,1)}), bf16[256,2048]{1,0:T(8,128)(2,1)}) %all-gather.6.cloned.1.call-update) | async-done | bytes 1048592 | tf_op jit(solution)/shard_map/all_gather | solution.py:21
  36.1 0.0 copy-start
  36.1 6.1 %convolution_convert_fusion.2 = bf16[256,2048]{1,0:T(8,128)(2,1)S(1)} fusion(bf16[256,2048]{1,0:T(8,128)(2,1)} %all-gather.6.cloned.1.call-done, bf16[2048,2048]{1,0:T(8,128)(2,1)} %param.8), kind=kOutput, calls=%fused_computation.7 | convolution fusion | flops 2148007936 | bytes 10485760 | tf_op jit(solution)/shard_map/dot_general | solution.py:27
  42.2 0.0 copy-done
  42.2 5.8 %convolution_convert_fusion.3 = bf16[256,2048]{1,0:T(8,128)(2,1)S(1)} fusion(bf16[256,2048]{1,0:T(8,128)(2,1)S(1)} %copy-done, bf16[2048,2048]{1,0:T(8,128)(2,1)} %param.7), kind=kOutput, calls=%fused_computation.8 | convolution fusion | flops 2148007936 | bytes 10485760 | tf_op jit(solution)/shard_map/dot_general | solution.py:26
  48.1 13.5 %all-gather.8.cloned.1.call-done = bf16[256,2048]{1,0:T(8,128)(2,1)} async-done(((bf16[32,2048]{1,0:T(8,128)(2,1)}), bf16[256,2048]{1,0:T(8,128)(2,1)}) %all-gather.8.cloned.1.call-update) | async-done | bytes 1048592 | tf_op jit(solution)/shard_map/all_gather | solution.py:22
  61.5 6.1 %convolution_convert_fusion.1 = bf16[256,2048]{1,0:T(8,128)(2,1)S(1)} fusion(bf16[256,2048]{1,0:T(8,128)(2,1)} %all-gather.8.cloned.1.call-done, bf16[2048,2048]{1,0:T(8,128)(2,1)} %param.9), kind=kOutput, calls=%fused_computation.6 | convolution fusion | flops 2148007936 | bytes 10485760 | tf_op jit(solution)/shard_map/dot_general | solution.py:28
  67.6 1.8 pad_maximum_fusion
  69.4 0.0 reduce-scatter.3.cloned.1.call-update
  69.4 0.0 all-gather.10.cloned.1.call-start
  69.5 60.4 %reduce-scatter.3.cloned.1.call-done = bf16[64,6144]{1,0:T(8,128)(2,1)} async-done(((bf16[256,6144]{1,0:T(8,128)(2,1)}), bf16[64,6144]{1,0:T(8,128)(2,1)}) %reduce-scatter.3.cloned.1.call-update) | async-done | bytes 786448 | tf_op jit(solution)/shard_map/reduce_scatter | solution.py:29
  129.8 1.2 convert_element_type.31
  131.1 1.1 multiply_convert_fusion
  132.2 0.0 all-gather.10.cloned.1.call-update
  132.2 0.0 all-gather.12.cloned.1.call-start
  132.3 0.5 all-gather.12.cloned.1.call-update
  132.8 0.0 all-gather.14.cloned.1.call-start
  132.9 0.5 all-gather.14.cloned.1.call-update
  133.4 0.2 reduce-scatter.5.cloned.1.call-start
  133.6 26.7 %all-gather.10.cloned.1.call-done = bf16[256,2048]{1,0:T(8,128)(2,1)} async-done(((bf16[64,2048]{1,0:T(8,128)(2,1)}), bf16[256,2048]{1,0:T(8,128)(2,1)}) %all-gather.10.cloned.1.call-update) | async-done | bytes 1048592 | tf_op jit(solution)/shard_map/all_gather | solution.py:38
  160.4 7.4 %fusion.2 = f32[256,2048]{1,0:T(8,128)} fusion(bf16[256,2048]{1,0:T(8,128)(2,1)} %all-gather.10.cloned.1.call-done, bf16[2048,2048]{1,0:T(8,128)(2,1)} %param.7), kind=kOutput, calls=%fused_computation.14 | convolution fusion | flops 2147483648 | bytes 11534336 | tf_op jit(solution)/shard_map/dot_general | solution.py:41
  167.8 22.0 %all-gather.12.cloned.1.call-done = bf16[256,2048]{1,0:T(8,128)(2,1)} async-done(((bf16[64,2048]{1,0:T(8,128)(2,1)}), bf16[256,2048]{1,0:T(8,128)(2,1)}) %all-gather.12.cloned.1.call-update) | async-done | bytes 1048592 | tf_op jit(solution)/shard_map/all_gather | solution.py:39
  189.8 0.0 copy-start.2
  189.8 7.7 %fusion = bf16[256,2048]{1,0:T(8,128)(2,1)} fusion(f32[256,2048]{1,0:T(8,128)} %fusion.2, bf16[256,2048]{1,0:T(8,128)(2,1)} %all-gather.12.cloned.1.call-done, bf16[2048,2048]{1,0:T(8,128)(2,1)} %param.8), kind=kOutput, calls=%fused_computation.5 | convolution fusion | flops 2148532224 | bytes 12582912 | tf_op jit(solution)/shard_map/dot_general | solution.py:43
  197.5 0.0 reduce-scatter.5.cloned.1.call-update
  197.6 0.0 copy-done.2
  197.6 5.8 %convert_bitcast_fusion = bf16[2048,2048]{0,1:T(8,128)(2,1)} fusion(bf16[256,2048]{1,0:T(8,128)(2,1)S(1)} %copy-done.2, bf16[256,2048]{1,0:T(8,128)(2,1)S(1)} %copy-done), kind=kOutput, calls=%fused_computation | convolution fusion | flops 2151677952 | bytes 10485760 | tf_op jit(solution)/shard_map/dot_general | solution.py:54
  203.3 0.0 copy-start.1
  203.3 12.3 %copy.10 = bf16[2048,2048]{1,0:T(8,128)(2,1)} copy(bf16[2048,2048]{0,1:T(8,128)(2,1)} %convert_bitcast_fusion) | data formatting | bytes 16777216
  215.7 0.0 copy-done.1
  215.7 5.8 %convert_bitcast_fusion.1 = bf16[2048,2048]{0,1:T(8,128)(2,1)} fusion(bf16[256,2048]{1,0:T(8,128)(2,1)S(1)} %copy-done.1, bf16[256,2048]{1,0:T(8,128)(2,1)S(1)} %copy-done), kind=kOutput, calls=%fused_computation.1 | convolution fusion | flops 2151677952 | bytes 10485760 | tf_op jit(solution)/shard_map/dot_general | solution.py:51
  221.5 0.0 copy-start.3
  221.5 12.4 %copy.9 = bf16[2048,2048]{1,0:T(8,128)(2,1)} copy(bf16[2048,2048]{0,1:T(8,128)(2,1)} %convert_bitcast_fusion.1) | data formatting | bytes 16777216
  233.8 0.0 all-gather.14.cloned.1.call-done
  233.8 0.0 copy-done.3
  233.8 7.0 %convolution_convert_fusion = bf16[2048,2048]{1,0:T(8,128)(2,1)} fusion(bf16[256,2048]{1,0:T(8,128)(2,1)} %all-gather.14.cloned.1.call-done, bf16[256,2048]{1,0:T(8,128)(2,1)S(1)} %copy-done.3), kind=kOutput, calls=%fused_computation.2 | convolution fusion | flops 2151677952 | bytes 10485760 | tf_op jit(solution)/shard_map/dot_general | solution.py:57
  240.8 17.2 %reduce-scatter.5.cloned.1.call-done = bf16[32,2048]{1,0:T(8,128)(2,1)} async-done(((bf16[256,2048]{1,0:T(8,128)(2,1)}), bf16[32,2048]{1,0:T(8,128)(2,1)}) %reduce-scatter.5.cloned.1.call-update) | async-done | bytes 131088 | tf_op jit(solution)/shard_map/reduce_scatter | solution.py:42
Async XLA Ops:
  7.2 28.9 %all-gather.6.cloned.1.call-start = ((), (), s32[]{:S(2)}) async-start(), calls=%async_computation.2 | async-start | bytes 1179648 | tf_op jit(solution)/shard_map/all_gather | solution.py:21
  7.9 53.6 %all-gather.8.cloned.1.call-start = ((), (), s32[]{:S(2)}) async-start(), calls=%async_computation.3 | async-start | bytes 1179648 | tf_op jit(solution)/shard_map/all_gather | solution.py:22
  8.6 121.2 %reduce-scatter.3.cloned.1.call-start = ((), (), s32[]{:S(2)}) async-start(), calls=%async_computation.4 | async-start | bytes 3932160 | tf_op jit(solution)/shard_map/reduce_scatter | solution.py:29
  36.1 6.1 %copy-start = (bf16[256,2048]{1,0:T(8,128)(2,1)S(1)}, bf16[256,2048]{1,0:T(8,128)(2,1)}, u32[]{:S(2)}) copy-start(bf16[256,2048]{1,0:T(8,128)(2,1)} %all-gather.6.cloned.1.call-done) | copy-start | bytes 3145732
  69.4 90.9 %all-gather.10.cloned.1.call-start = ((), (), s32[]{:S(2)}) async-start(), calls=%async_computation.5 | async-start | bytes 1310720 | tf_op jit(solution)/shard_map/all_gather | solution.py:38
  132.2 57.6 %all-gather.12.cloned.1.call-start = ((), (), s32[]{:S(2)}) async-start(), calls=%async_computation.6 | async-start | bytes 1310720 | tf_op jit(solution)/shard_map/all_gather | solution.py:39
  132.8 101.0 %all-gather.14.cloned.1.call-start = ((), (), s32[]{:S(2)}) async-start(), calls=%async_computation.8 | async-start | bytes 1310720 | tf_op jit(solution)/shard_map/all_gather | solution.py:37
  133.4 124.6 %reduce-scatter.5.cloned.1.call-start = ((), (), s32[]{:S(2)}) async-start(), calls=%async_computation.7 | async-start | bytes 1179648 | tf_op jit(solution)/shard_map/reduce_scatter | solution.py:42
  189.8 7.7 %copy-start.2 = (bf16[256,2048]{1,0:T(8,128)(2,1)S(1)}, bf16[256,2048]{1,0:T(8,128)(2,1)}, u32[]{:S(2)}) copy-start(bf16[256,2048]{1,0:T(8,128)(2,1)} %all-gather.12.cloned.1.call-done) | copy-start | bytes 3145732
  203.3 12.3 %copy-start.1 = (bf16[256,2048]{1,0:T(8,128)(2,1)S(1)}, bf16[256,2048]{1,0:T(8,128)(2,1)}, u32[]{:S(2)}) copy-start(bf16[256,2048]{1,0:T(8,128)(2,1)} %all-gather.10.cloned.1.call-done) | copy-start | bytes 3145732
  221.5 12.4 %copy-start.3 = (bf16[256,2048]{1,0:T(8,128)(2,1)S(1)}, bf16[256,2048]{1,0:T(8,128)(2,1)}, u32[]{:S(2)}) copy-start(bf16[256,2048]{1,0:T(8,128)(2,1)} %all-gather.8.cloned.1.call-done) | copy-start | bytes 3145732
Sparse Core Ops, SparseCore 0:
  9.9 26.1 all-gather.5
  38.0 23.4 all-gather.7
  69.6 60.2 reduce-scatter.2
  132.4 27.9 all-gather.9
  162.3 27.4 all-gather.11
  191.2 27.4 all-gather.13
  222.4 35.5 reduce-scatter.4
where the time goes:
time: 266 us; the launch traced here: 265 us
  waiting for transfers between devices  170 us (64%)
  matrix products  51.7 us (19%)
  local copies, waits for them, and re-layouts  24.7 us (9%)
  between operations  14.2 us (5%)
  other arithmetic  4.18 us (2%)
    reduce_scatter x1, waiting for transfers between devices, on_device(): lax.psum_scatter(jnp.concatenate([gate, up, back], axis=1).astype(jnp.bfl...  60.4 us
    all_gather x1, waiting for transfers between devices, on_device(): lax.all_gather(inputs, 'col', axis=0, tiled=True)  27.4 us
    all_gather x1, waiting for transfers between devices, on_device(): lax.all_gather(gate_delta, 'row', axis=0, tiled=True)  26.7 us
    unnamed x10, local copies, waits for them, and re-layouts  24.7 us
    all_gather x1, waiting for transfers between devices, on_device(): lax.all_gather(up_delta, 'row', axis=0, tiled=True)  22 us
    reduce_scatter x1, waiting for transfers between devices, on_device(): lax.psum_scatter((first + lax.dot_general(up_all, w_up, rest, preferred_e...  17.2 us
    all_gather x1, waiting for transfers between devices, on_device(): lax.all_gather(out_grad, 'col', axis=0, tiled=True)  13.5 us
    dot_general x1, matrix products, on_device(): lax.dot_general(up_all, w_up, rest, preferred_element_type=jnp.float32)  7.71 us
  transfers between devices with their start and end apart: 7, of which 6 were waited for; matrix products, arithmetic and copies ran while one was open for 27% of the time, Pallas kernels for 0%

commit v1 on v0

v1 whole, which is shorter than its diff:
```python
import functools

import jax
import jax.numpy as jnp
from jax import lax
from jax.experimental import pallas as pl
from jax.experimental.pallas import tpu as pltpu
from jax.sharding import PartitionSpec as P

MESH = pl.DeviceIdType.MESH
BF16, F32 = jnp.bfloat16, jnp.float32
REST = (((1,), (1,)), ((), ()))


def remote(src, dst, send, recv, device):
    return pltpu.make_async_remote_copy(
        src_ref=src, dst_ref=dst, send_sem=send, recv_sem=recv, device_id=device, device_id_type=MESH
    )


def kernel(
    nr, nc, fc,
    x_ref, g_ref, wg_ref, wu_ref, wd_ref,
    ig_ref, xo_ref, go_ref, ho_ref, gdo_ref, udo_ref,
    xg, wgu, wdv, part, inb, exb, res, acc, pair_out, pair_in, sum_out, chip_in,
    own_sem, w_sem, ag_send, ag_recv, fw_send, in_send, in_recv, ex_recv, res_send, res_recv,
    out_sem, act_sem, pair_send, pair_recv, chip_send, chip_recv,
):
    row, col = lax.axis_index("row"), lax.axis_index("col")
    tl, dl = x_ref.shape
    nch = wgu.shape[0]
    chips = nc // 2
    core, chip = lax.rem(col, 2), col // 2
    sibling = chip * 2 + 1 - core
    half = nr // 2
    low = row < half
    inward = jnp.where(low, row + 1, row - 1)
    outward = jnp.where(low, row - 1, row + 1)
    mid = jnp.logical_or(row == half - 1, row == half)
    edge = jnp.logical_or(row == 0, row == nr - 1)
    not_mid, not_edge = jnp.logical_not(mid), jnp.logical_not(edge)

    def peer(k):
        return lax.rem(chip + k, chips) * 2 + core

    def source(k):
        return lax.rem(chip + chips - k, chips) * 2 + core

    def tokens(b):
        return pl.ds(pl.multiple_of(b * tl, tl), tl)

    def hid(c):
        return pl.ds(pl.multiple_of(c * fc, fc), fc)

    def weights(c):
        return (
            pltpu.make_async_copy(wg_ref.at[:, hid(c)], wgu.at[c, :, pl.ds(0, fc)], w_sem.at[0, c]),
            pltpu.make_async_copy(wu_ref.at[:, hid(c)], wgu.at[c, :, pl.ds(fc, fc)], w_sem.at[1, c]),
            pltpu.make_async_copy(wd_ref.at[hid(c), :], wdv.at[c], w_sem.at[2, c]),
        )

    blocks = (x_ref, g_ref)

    def own(a):
        return pltpu.make_async_copy(blocks[a], xg.at[a, tokens(col), :], own_sem.at[a])

    for a in range(2):
        own(a).start()

    barrier = pltpu.get_barrier_semaphore()
    pl.semaphore_signal(barrier, inc=1, device_id=(row, sibling), device_id_type=MESH)
    for k in range(1, chips):
        pl.semaphore_signal(barrier, inc=1, device_id=(row, peer(k)), device_id_type=MESH)
    pl.semaphore_signal(barrier, inc=1, device_id=(inward, col), device_id_type=MESH)

    @pl.when(not_edge)
    def _():
        pl.semaphore_signal(barrier, inc=1, device_id=(outward, col), device_id_type=MESH)

    pl.semaphore_wait(barrier, chips + 1 + jnp.where(edge, 0, 1))

    def direct(a, k):
        to = peer(k) if k else sibling
        return remote(
            blocks[a], xg.at[a, tokens(col), :], ag_send.at[a, k], ag_recv.at[a, col], (row, to)
        )

    def forward(a, k):
        rows = tokens(source(k))
        return remote(
            xg.at[a, rows, :], xg.at[a, rows, :], fw_send.at[a, k], ag_recv.at[a, source(k)], (row, sibling)
        )

    def arrived(a, b):
        rows = tokens(b)
        return remote(xg.at[a, rows, :], xg.at[a, rows, :], fw_send.at[a, 0], ag_recv.at[a, b], (row, sibling))

    for a in range(2):
        for k in list(range(1, chips)) + [0]:
            direct(a, k).start()

    def load(c, _):
        for copy in weights(c):
            copy.start()
        return 0

    lax.fori_loop(0, nch, load, 0)
    acc[...] = jnp.zeros_like(acc)

    for a in range(2):
        own(a).wait()
        for k in range(1, chips):
            arrived(a, source(k)).wait_recv()
            forward(a, k).start()
    for a in range(2):
        arrived(a, sibling).wait_recv()
        for k in range(1, chips):
            arrived(a, source(k) + 1 - 2 * core).wait_recv()

    acts = (
        pltpu.make_async_copy(xg.at[0], xo_ref, act_sem.at[0]),
        pltpu.make_async_copy(xg.at[1], go_ref, act_sem.at[1]),
    )
    for copy in acts:
        copy.start()

    def inner(c):
        return remote(part.at[c], inb.at[c], in_send.at[c], in_recv.at[c], (inward, col))

    def exchange(c):
        return remote(part.at[c], exb.at[c], in_send.at[c], ex_recv.at[c], (inward, col))

    def result(c):
        return remote(res.at[c], res.at[c], res_send.at[c], res_recv.at[c], (outward, col))

    def outs(c):
        return (
            pltpu.make_async_copy(res.at[c, :, pl.ds(0, fc)], ho_ref.at[:, hid(c)], out_sem.at[0, c]),
            pltpu.make_async_copy(res.at[c, :, pl.ds(fc, fc)], gdo_ref.at[:, hid(c)], out_sem.at[1, c]),
            pltpu.make_async_copy(res.at[c, :, pl.ds(2 * fc, fc)], udo_ref.at[:, hid(c)], out_sem.at[2, c]),
        )

    def back(c):
        for copy in outs(c):
            copy.start()
        deltas = res[c, :, fc:]
        piece = min(512, dl)
        for p in range(dl // piece):
            cols = slice(p * piece, (p + 1) * piece)
            acc[:, cols] += lax.dot_general(deltas, wgu[c, cols, :], REST, preferred_element_type=F32)

    def step(c, _):
        @pl.when(c < nch)
        def _():
            for copy in weights(c):
                copy.wait()
            part[c, :, : 2 * fc] = jnp.dot(xg[0], wgu[c], preferred_element_type=F32).astype(BF16)
            part[c, :, 2 * fc :] = lax.dot_general(
                xg[1], wdv[c], REST, preferred_element_type=F32
            ).astype(BF16)

            @pl.when(not_edge)
            def _():
                inner(c).wait_recv()
                part[c] = (part[c].astype(F32) + inb[c].astype(F32)).astype(BF16)

            @pl.when(mid)
            def _():
                exchange(c).start()

            @pl.when(not_mid)
            def _():
                inner(c).start()

        @pl.when(jnp.logical_and(mid, c > 0))
        def _():
            b = c - 1
            exchange(b).wait_recv()

            def summed(i):
                cols = slice(i * fc, (i + 1) * fc)
                return part[b, :, cols].astype(F32) + exb[b, :, cols].astype(F32)

            gate, up, grad = summed(0), summed(1), summed(2)
            sig = jax.nn.sigmoid(gate)
            act = gate * sig
            res[b, :, :fc] = (act * up).astype(BF16)
            res[b, :, fc : 2 * fc] = (grad * up * sig * (1.0 + gate * (1.0 - sig))).astype(BF16)
            res[b, :, 2 * fc :] = (grad * act).astype(BF16)

            @pl.when(not_edge)
            def _():
                result(b).start()

            back(b)

        return 0

    lax.fori_loop(0, nch + 1, step, 0)

    @pl.when(not_mid)
    def _():
        def take(c, _):
            result(c).wait_recv()

            @pl.when(not_edge)
            def _():
                result(c).start()

            back(c)
            return 0

        lax.fori_loop(0, nch, take, 0)

    def pair(j):
        return remote(
            pair_out.at[j], pair_in.at[j], pair_send.at[j], pair_recv.at[j], (row, sibling)
        )

    def across(j, owner):
        return remote(
            sum_out.at[j], chip_in.at[chip], chip_send.at[j], chip_recv.at[chip], (row, owner)
        )

    order = [lax.rem(chip + k, chips) for k in list(range(1, chips)) + [0]]
    for j in order:
        pair_out[j] = acc[tokens(2 * j + 1 - core), :].astype(BF16)
        pair(j).start()
    for j in order[:-1]:
        pair(j).wait_recv()
        sum_out[j] = (acc[tokens(2 * j + core), :] + pair_in[j].astype(F32)).astype(BF16)
        across(j, 2 * j + core).start()
    pair(chip).wait_recv()
    total = acc[tokens(col), :] + pair_in[chip].astype(F32)
    for j in order[:-1]:
        remote(sum_out.at[j], chip_in.at[j], chip_send.at[j], chip_recv.at[j], (row, 2 * j + core)).wait_recv()
        total = total + chip_in[j].astype(F32)
    ig_ref[...] = total.astype(BF16)

    for a in range(2):
        for k in range(chips):
            direct(a, k).wait_send()
        for k in range(1, chips):
            forward(a, k).wait_send()
        acts[a].wait()

    def drain(c, _):
        inner(c).wait_send()

        @pl.when(not_edge)
        def _():
            result(c).wait_send()

        for copy in outs(c):
            copy.wait()
        return 0

    lax.fori_loop(0, nch, drain, 0)
    for j in order:
        pair(j).wait_send()
    for j in order[:-1]:
        across(j, 2 * j + core).wait_send()


def on_device(nr, nc, x, g, wg, wu, wd):
    tl, dl = x.shape
    fl = wg.shape[1]
    rows = tl * nc
    fc = min(128, fl)
    nch = fl // fc
    chips = nc // 2
    dma = pltpu.SemaphoreType.DMA
    any_spec = pl.BlockSpec(memory_space=pl.ANY)
    acts = jax.ShapeDtypeStruct((rows, dl), BF16)
    hids = jax.ShapeDtypeStruct((rows, fl), BF16)
    flops = 10 * rows * dl * fl
    grad, x_all, g_all, hidden, gate_delta, up_delta = pl.pallas_call(
        functools.partial(kernel, nr, nc, fc),
        out_shape=(jax.ShapeDtypeStruct((tl, dl), BF16), acts, acts, hids, hids, hids),
        in_specs=[any_spec] * 5,
        out_specs=(pl.BlockSpec(memory_space=pltpu.VMEM),) + (any_spec,) * 5,
        scratch_shapes=[
            pltpu.VMEM((2, rows, dl), BF16),
            pltpu.VMEM((nch, dl, 2 * fc), BF16),
            pltpu.VMEM((nch, fc, dl), BF16),
            pltpu.VMEM((nch, rows, 3 * fc), BF16),
            pltpu.VMEM((nch, rows, 3 * fc), BF16),
            pltpu.VMEM((nch, rows, 3 * fc), BF16),
            pltpu.VMEM((nch, rows, 3 * fc), BF16),
            pltpu.VMEM((rows, dl), F32),
            pltpu.VMEM((chips, tl, dl), BF16),
            pltpu.VMEM((chips, tl, dl), BF16),
            pltpu.VMEM((chips, tl, dl), BF16),
            pltpu.VMEM((chips, tl, dl), BF16),
            dma((2,)),
            dma((3, nch)),
            dma((2, chips)),
            dma((2, nc)),
            dma((2, chips)),
            dma((nch,)),
            dma((nch,)),
            dma((nch,)),
            dma((nch,)),
            dma((nch,)),
            dma((3, nch)),
            dma((2,)),
            dma((chips,)),
            dma((chips,)),
            dma((chips,)),
            dma((chips,)),
        ],
        compiler_params=pltpu.CompilerParams(
            collective_id=0, has_side_effects=True, vmem_limit_bytes=56 * 2**20
        ),
        cost_estimate=pl.CostEstimate(flops=flops, bytes_accessed=6 * dl * fl, transcendentals=rows * fl),
    )(x, g, wg, wu, wd)
    contract = (((0,), (0,)), ((), ()))

    def wgrad(a, b):
        return lax.dot_general(a, b, contract, preferred_element_type=F32).astype(BF16)

    return grad, wgrad(x_all, gate_delta), wgrad(x_all, up_delta), wgrad(hidden, g_all)


def solution(mesh):
    in_specs = (P("col", "row"), P("col", "row"), P("row", "col"), P("row", "col"), P("col", "row"))
    out_specs = (P("col", "row"), P("row", "col"), P("row", "col"), P("col", "row"))
    return jax.shard_map(
        functools.partial(on_device, mesh.shape["row"], mesh.shape["col"]),
        mesh=mesh, in_specs=in_specs, out_specs=out_specs, check_vma=False,
    )
```

time: 266 us -> 134 us (0.50)
  waiting for transfers between devices: 170 us -> 0 us
  Pallas kernels: 0 us -> 114 us
  matrix products: 51.7 us -> 19 us
  local copies, waits for them, and re-layouts: 24.7 us -> 0.68 us
  between operations: 14.2 us -> 0.67 us
  other arithmetic: 4.18 us -> 0 us
    pallas_call x0 -> x1, Pallas kernels: none -> 114 us  [on_device(): pl.pallas_call(functools.partial(kernel, nr, nc, fc), out_shape=(jax.Shap...]
    all_gather x5 -> x0, waiting for transfers between devices: 89.6 us -> none  [the longest x1 27.4 us: on_device(): lax.all_gather(inputs, 'col', axis=0, tiled=True)]
    reduce_scatter x2 -> x0, waiting for transfers between devices: 77.5 us -> none  [the longest x1 60.4 us: on_device(): lax.psum_scatter(jnp.concatenate([gate, up, back], axis=1).astype(jnp.bfl...]
    dot_general x8 -> x3, matrix products: 51.7 us -> 19 us  [wgrad(): lax.dot_general(a, b, contract, preferred_element_type=F32).astype(BF16)]
    unnamed x10 -> x11, local copies, waits for them, and re-layouts: 24.7 us -> 0.68 us
  transfers between devices with their start and end apart: 7 -> 0, of which waited for: 6 -> 0; matrix products, arithmetic and copies ran while one was open for 27% -> 0% of each run, Pallas kernels for 0% -> 0%
where the time goes in v1:
time: 134 us
  Pallas kernels  114 us (85%)
  matrix products  19 us (14%)
    pallas_call x1, Pallas kernels, on_device(): pl.pallas_call(functools.partial(kernel, nr, nc, fc), out_shape=(jax.Shap...  114 us
    dot_general x3, matrix products, wgrad(): lax.dot_general(a, b, contract, preferred_element_type=F32).astype(BF16)  19 us

profile of v1, /device:TPU:0, one launch (start us, length us, event | category | flops | bytes accessed | tf_op | source)
XLA Modules:
  0.0 134.1 jit_solution(10930261674649994701)
XLA Ops:
  0.6 113.7 %shard_map.84 = (bf16[32,2048]{1,0:T(8,128)(2,1)}, bf16[256,2048]{1,0:T(8,128)(2,1)}, bf16[256,2048]{1,0:T(8,128)(2,1)}, bf16[256,2048]{1,0:T(8,128)(2,1)}, bf16...) custom-call(bf16[32,2048]{1,0:T(8,128)(2,1)} %x_ref.1, bf16[32,2048]{1,0:T(8,128)(2,1)} %g_ref.1, ...), custom_call_target="tpu_custom_call" | custom-call | flops 10737418240 | bytes 25165824 | tf_op jit(solution)/shard_map/pallas_call | solution.py:277
  114.3 0.0 copy-start
  114.3 0.0 copy-start.3
  114.3 7.5 %convolution_convert_fusion.2 = bf16[2048,2048]{1,0:T(8,128)(2,1)} fusion(bf16[256,2048]{1,0:T(8,128)(2,1)} %get-tuple-element.11, bf16[256,2048]{1,0:T(8,128)(2,1)} %get-tuple-element.12), kind=kOutput, calls=%fused_computation.2 | convolution fusion | flops 2151677952 | bytes 10485760 | tf_op jit(solution)/shard_map/dot_general | solution.py:320
  121.8 0.0 copy-done
  121.8 0.0 copy-done.3
  121.8 0.0 copy-start.1
  121.8 0.0 copy-start.2
  121.8 5.8 %convolution_convert_fusion.1 = bf16[2048,2048]{1,0:T(8,128)(2,1)} fusion(bf16[256,2048]{1,0:T(8,128)(2,1)S(1)} %copy-done, bf16[256,2048]{1,0:T(8,128)(2,1)S(1)} %copy-done.3), kind=kOutput, calls=%fused_computation.1 | convolution fusion | flops 2151677952 | bytes 10485760 | tf_op jit(solution)/shard_map/dot_general | solution.py:320
  127.6 0.0 copy-done.1
  127.6 0.0 copy-done.2
  127.6 0.0 copy-start.4
  127.6 5.8 %convolution_convert_fusion = bf16[2048,2048]{1,0:T(8,128)(2,1)} fusion(bf16[256,2048]{1,0:T(8,128)(2,1)S(1)} %copy-done.1, bf16[256,2048]{1,0:T(8,128)(2,1)S(1)} %copy-done.2), kind=kOutput, calls=%fused_computation | convolution fusion | flops 2151677952 | bytes 10485760 | tf_op jit(solution)/shard_map/dot_general | solution.py:320
  133.4 0.0 copy-done.4
  133.4 0.7 copy.10
Async XLA Ops:
  114.3 7.5 %copy-start = (bf16[256,2048]{1,0:T(8,128)(2,1)S(1)}, bf16[256,2048]{1,0:T(8,128)(2,1)}, u32[]{:S(2)}) copy-start(bf16[256,2048]{1,0:T(8,128)(2,1)} %get-tuple-element.11) | copy-start | bytes 3145732
  114.3 7.5 %copy-start.3 = (bf16[256,2048]{1,0:T(8,128)(2,1)S(1)}, bf16[256,2048]{1,0:T(8,128)(2,1)}, u32[]{:S(2)}) copy-start(bf16[256,2048]{1,0:T(8,128)(2,1)} %get-tuple-element.13) | copy-start | bytes 3145732
  121.8 5.8 %copy-start.1 = (bf16[256,2048]{1,0:T(8,128)(2,1)S(1)}, bf16[256,2048]{1,0:T(8,128)(2,1)}, u32[]{:S(2)}) copy-start(bf16[256,2048]{1,0:T(8,128)(2,1)} %get-tuple-element.14) | copy-start | bytes 3145732
  121.8 5.8 %copy-start.2 = (bf16[256,2048]{1,0:T(8,128)(2,1)S(1)}, bf16[256,2048]{1,0:T(8,128)(2,1)}, u32[]{:S(2)}) copy-start(bf16[256,2048]{1,0:T(8,128)(2,1)} %get-tuple-element.15) | copy-start | bytes 3145732
  127.6 5.8 %copy-start.4 = (bf16[32,2048]{1,0:T(8,128)(2,1)S(1)}, bf16[32,2048]{1,0:T(8,128)(2,1)}, u32[]{:S(2)}) copy-start(bf16[32,2048]{1,0:T(8,128)(2,1)} %get-tuple-element.20) | copy-start | bytes 393220

commit v2 on v1

v2 whole, which is shorter than its diff:
```python
import functools

import jax
import jax.numpy as jnp
from jax import lax
from jax.experimental import pallas as pl
from jax.experimental.pallas import tpu as pltpu
from jax.sharding import PartitionSpec as P

MESH = pl.DeviceIdType.MESH
BF16, F32 = jnp.bfloat16, jnp.float32
REST = (((1,), (1,)), ((), ()))
LAG = 2


def remote(src, dst, send, recv, device):
    return pltpu.make_async_remote_copy(
        src_ref=src, dst_ref=dst, send_sem=send, recv_sem=recv, device_id=device, device_id_type=MESH
    )


def kernel(
    nr, nc, fc,
    x_ref, g_ref, wg_ref, wu_ref, wd_ref,
    ig_ref, xo_ref, go_ref, ho_ref, gdo_ref, udo_ref,
    xg, wgu, wdv, part, inb, exb, res, acc, pair_out, pair_in, sum_out, chip_in,
    own_sem, w_sem, ag_send, ag_recv, fw_send, in_send, in_recv, ex_recv, res_send, res_recv,
    out_sem, act_sem, pair_send, pair_recv, chip_send, chip_recv,
):
    row, col = lax.axis_index("row"), lax.axis_index("col")
    tl, dl = x_ref.shape
    nch = wgu.shape[0]
    chips = nc // 2
    tg = 2 * tl
    units = chips * nch
    core, chip = lax.rem(col, 2), col // 2
    sibling = chip * 2 + 1 - core
    half = nr // 2
    low = row < half
    inward = jnp.where(low, row + 1, row - 1)
    outward = jnp.where(low, row - 1, row + 1)
    mid = jnp.logical_or(row == half - 1, row == half)
    edge = jnp.logical_or(row == 0, row == nr - 1)
    not_mid, not_edge = jnp.logical_not(mid), jnp.logical_not(edge)
    mine = pl.ds(pl.multiple_of(core * tl, tl), tl)
    other = pl.ds(pl.multiple_of((1 - core) * tl, tl), tl)
    blocks = (x_ref, g_ref)

    def peer(k):
        return lax.rem(chip + k, chips) * 2 + core

    def owner(k):
        return lax.rem(chip + chips - k, chips) * 2 + core

    def hid(c):
        return pl.ds(pl.multiple_of(c * fc, fc), fc)

    def weights(c):
        return (
            pltpu.make_async_copy(wg_ref.at[:, hid(c)], wgu.at[c, :, pl.ds(0, fc)], w_sem.at[0, c]),
            pltpu.make_async_copy(wu_ref.at[:, hid(c)], wgu.at[c, :, pl.ds(fc, fc)], w_sem.at[1, c]),
            pltpu.make_async_copy(wd_ref.at[hid(c), :], wdv.at[c], w_sem.at[2, c]),
        )

    def own(a):
        return pltpu.make_async_copy(blocks[a], xg.at[a, 0, mine, :], own_sem.at[a])

    for a in range(2):
        own(a).start()

    barrier = pltpu.get_barrier_semaphore()
    pl.semaphore_signal(barrier, inc=1, device_id=(row, sibling), device_id_type=MESH)
    for k in range(1, chips):
        pl.semaphore_signal(barrier, inc=1, device_id=(row, peer(k)), device_id_type=MESH)
    pl.semaphore_signal(barrier, inc=1, device_id=(inward, col), device_id_type=MESH)

    @pl.when(not_edge)
    def _():
        pl.semaphore_signal(barrier, inc=1, device_id=(outward, col), device_id_type=MESH)

    for copy in weights(0):
        copy.start()
    pl.semaphore_wait(barrier, chips + 1 + jnp.where(edge, 0, 1))

    def direct(a, k):
        return remote(
            blocks[a], xg.at[a, k, mine, :], ag_send.at[a, k], ag_recv.at[a, k, 0],
            (row, peer(k) if k else sibling),
        )

    def came(a, k):
        return remote(
            xg.at[a, k, mine, :], xg.at[a, k, mine, :], fw_send.at[a, k], ag_recv.at[a, k, 0], (row, sibling)
        )

    def forward(a, k):
        return remote(
            xg.at[a, k, mine, :], xg.at[a, k, mine, :], fw_send.at[a, k], ag_recv.at[a, k, 1], (row, sibling)
        )

    def forwarded(a, k):
        return remote(
            xg.at[a, k, other, :], xg.at[a, k, other, :], fw_send.at[a, k], ag_recv.at[a, k, 1], (row, sibling)
        )

    for k in range(chips):
        for a in range(2):
            direct(a, k).start()

    def load(c, _):
        for copy in weights(c):
            copy.start()
        return 0

    lax.fori_loop(1, nch, load, 0)
    acc[...] = jnp.zeros_like(acc)

    for a in range(2):
        own(a).wait()
        remote(
            xg.at[a, 0, other, :], xg.at[a, 0, other, :], fw_send.at[a, 0], ag_recv.at[a, 0, 0], (row, sibling)
        ).wait_recv()

    def inner(u):
        return remote(part.at[u], inb.at[u], in_send.at[u], in_recv.at[u], (inward, col))

    def exchange(u):
        return remote(part.at[u], exb.at[u], in_send.at[u], ex_recv.at[u], (inward, col))

    def result(u):
        return remote(res.at[u], res.at[u], res_send.at[u], res_recv.at[u], (outward, col))

    def outs(u):
        k, c = u // nch, lax.rem(u, nch)
        rows = pl.ds(pl.multiple_of(k * tg, tg), tg)
        return [
            pltpu.make_async_copy(
                res.at[u, :, pl.ds(i * fc, fc)], ref.at[rows, hid(c)], out_sem.at[i, u]
            )
            for i, ref in enumerate((ho_ref, gdo_ref, udo_ref))
        ]

    def pair(k):
        return remote(
            pair_out.at[k], pair_in.at[k], pair_send.at[k], pair_recv.at[k], (row, sibling)
        )

    def across(k):
        return remote(
            sum_out.at[k], chip_in.at[k], chip_send.at[k], chip_recv.at[k], (row, owner(k))
        )

    def settle(k):
        pair(k).wait_recv()
        sum_out[k] = (acc[k, mine, :] + pair_in[k].astype(F32)).astype(BF16)
        across(k).start()

    def back(u):
        k, c = u // nch, lax.rem(u, nch)
        for copy in outs(u):
            copy.start()
        deltas = res[u, :, fc:]
        piece = min(512, dl)
        for p in range(dl // piece):
            cols = slice(p * piece, (p + 1) * piece)
            acc[k, :, cols] += lax.dot_general(deltas, wgu[c, cols, :], REST, preferred_element_type=F32)

        @pl.when(jnp.logical_and(c == nch // 2, k > 1))
        def _():
            settle(k - 1)

        @pl.when(c == nch - 1)
        def _():
            pair_out[k] = acc[k, other, :].astype(BF16)
            pair(k).start()

    def step(u, _):
        @pl.when(u < units)
        def _():
            k, c = u // nch, lax.rem(u, nch)

            @pl.when(k == 0)
            def _():
                for copy in weights(c):
                    copy.wait()

            @pl.when(jnp.logical_and(k > 0, c == 0))
            def _():
                for a in range(2):
                    forwarded(a, k).wait_recv()

            part[u, :, : 2 * fc] = jnp.dot(xg[0, k], wgu[c], preferred_element_type=F32).astype(BF16)
            part[u, :, 2 * fc :] = lax.dot_general(
                xg[1, k], wdv[c], REST, preferred_element_type=F32
            ).astype(BF16)

            @pl.when(not_edge)
            def _():
                inner(u).wait_recv()
                part[u] = (part[u].astype(F32) + inb[u].astype(F32)).astype(BF16)

            @pl.when(mid)
            def _():
                exchange(u).start()

            @pl.when(not_mid)
            def _():
                inner(u).start()

            @pl.when(jnp.logical_and(c == nch // 2, k + 1 < chips))
            def _():
                for a in range(2):
                    came(a, k + 1).wait_recv()
                    forward(a, k + 1).start()

        @pl.when(jnp.logical_and(mid, u >= LAG))
        def _():
            v = u - LAG
            exchange(v).wait_recv()

            def summed(i):
                cols = slice(i * fc, (i + 1) * fc)
                return part[v, :, cols].astype(F32) + exb[v, :, cols].astype(F32)

            gate, up, grad = summed(0), summed(1), summed(2)
            sig = jax.nn.sigmoid(gate)
            act = gate * sig
            res[v, :, :fc] = (act * up).astype(BF16)
            res[v, :, fc : 2 * fc] = (grad * up * sig * (1.0 + gate * (1.0 - sig))).astype(BF16)
            res[v, :, 2 * fc :] = (grad * act).astype(BF16)

            @pl.when(not_edge)
            def _():
                result(v).start()

            back(v)

        return 0

    lax.fori_loop(0, units + LAG, step, 0)

    acts = (
        pltpu.make_async_copy(xg.at[0], xo_ref, act_sem.at[0]),
        pltpu.make_async_copy(xg.at[1], go_ref, act_sem.at[1]),
    )
    for copy in acts:
        copy.start()

    @pl.when(not_mid)
    def _():
        def take(u, _):
            result(u).wait_recv()

            @pl.when(not_edge)
            def _():
                result(u).start()

            back(u)
            return 0

        lax.fori_loop(0, units, take, 0)

    if chips > 1:
        settle(chips - 1)
    pair(0).wait_recv()
    total = acc[0, mine, :] + pair_in[0].astype(F32)
    for k in range(1, chips):
        across(k).wait_recv()
        total = total + chip_in[k].astype(F32)
    ig_ref[...] = total.astype(BF16)

    for a in range(2):
        for k in range(chips):
            direct(a, k).wait_send()
        for k in range(1, chips):
            forward(a, k).wait_send()
        acts[a].wait()

    def drain(u, _):
        inner(u).wait_send()

        @pl.when(not_edge)
        def _():
            result(u).wait_send()

        for copy in outs(u):
            copy.wait()
        return 0

    lax.fori_loop(0, units, drain, 0)
    for k in range(chips):
        pair(k).wait_send()
    for k in range(1, chips):
        across(k).wait_send()


def on_device(nr, nc, x, g, wg, wu, wd):
    tl, dl = x.shape
    fl = wg.shape[1]
    rows = tl * nc
    fc = min(256, fl)
    nch = fl // fc
    chips = nc // 2
    tg = 2 * tl
    units = chips * nch
    dma = pltpu.SemaphoreType.DMA
    any_spec = pl.BlockSpec(memory_space=pl.ANY)
    acts = jax.ShapeDtypeStruct((chips, tg, dl), BF16)
    hids = jax.ShapeDtypeStruct((rows, fl), BF16)
    flops = 10 * rows * dl * fl
    grad, x_all, g_all, hidden, gate_delta, up_delta = pl.pallas_call(
        functools.partial(kernel, nr, nc, fc),
        out_shape=(jax.ShapeDtypeStruct((tl, dl), BF16), acts, acts, hids, hids, hids),
        in_specs=[any_spec] * 5,
        out_specs=(pl.BlockSpec(memory_space=pltpu.VMEM),) + (any_spec,) * 5,
        scratch_shapes=[
            pltpu.VMEM((2, chips, tg, dl), BF16),
            pltpu.VMEM((nch, dl, 2 * fc), BF16),
            pltpu.VMEM((nch, fc, dl), BF16),
            pltpu.VMEM((units, tg, 3 * fc), BF16),
            pltpu.VMEM((units, tg, 3 * fc), BF16),
            pltpu.VMEM((units, tg, 3 * fc), BF16),
            pltpu.VMEM((units, tg, 3 * fc), BF16),
            pltpu.VMEM((chips, tg, dl), F32),
            pltpu.VMEM((chips, tl, dl), BF16),
            pltpu.VMEM((chips, tl, dl), BF16),
            pltpu.VMEM((chips, tl, dl), BF16),
            pltpu.VMEM((chips, tl, dl), BF16),
            dma((2,)),
            dma((3, nch)),
            dma((2, chips)),
            dma((2, chips, 2)),
            dma((2, chips)),
            dma((units,)),
            dma((units,)),
            dma((units,)),
            dma((units,)),
            dma((units,)),
            dma((3, units)),
            dma((2,)),
            dma((chips,)),
            dma((chips,)),
            dma((chips,)),
            dma((chips,)),
        ],
        compiler_params=pltpu.CompilerParams(
            collective_id=0, has_side_effects=True, vmem_limit_bytes=56 * 2**20
        ),
        cost_estimate=pl.CostEstimate(flops=flops, bytes_accessed=6 * dl * fl, transcendentals=rows * fl),
    )(x, g, wg, wu, wd)
    x_all, g_all = x_all.reshape(rows, dl), g_all.reshape(rows, dl)
    contract = (((0,), (0,)), ((), ()))

    def wgrad(a, b):
        return lax.dot_general(a, b, contract, preferred_element_type=F32).astype(BF16)

    return grad, wgrad(x_all, gate_delta), wgrad(x_all, up_delta), wgrad(hidden, g_all)


def solution(mesh):
    in_specs = (P("col", "row"), P("col", "row"), P("row", "col"), P("row", "col"), P("col", "row"))
    out_specs = (P("col", "row"), P("row", "col"), P("row", "col"), P("col", "row"))
    return jax.shard_map(
        functools.partial(on_device, mesh.shape["row"], mesh.shape["col"]),
        mesh=mesh, in_specs=in_specs, out_specs=out_specs, check_vma=False,
    )
```

time: 134 us -> 115 us (0.86)
  Pallas kernels: 114 us -> 94.6 us
    pallas_call x1, Pallas kernels: 114 us -> 94.6 us  [on_device(): pl.pallas_call(functools.partial(kernel, nr, nc, fc), out_shape=(jax.Shap...]
where the time goes in v2:
time: 115 us
  Pallas kernels  94.6 us (82%)
  matrix products  19 us (17%)
    pallas_call x1, Pallas kernels, on_device(): pl.pallas_call(functools.partial(kernel, nr, nc, fc), out_shape=(jax.Shap...  94.6 us
    dot_general x3, matrix products, wgrad(): lax.dot_general(a, b, contract, preferred_element_type=F32).astype(BF16)  19 us

profile of v2, /device:TPU:0, one launch (start us, length us, event | category | flops | bytes accessed | tf_op | source)
XLA Modules:
  0.0 115.0 jit_solution(2774160394957719142)
XLA Ops:
  0.6 94.6 %shard_map.84 = (bf16[32,2048]{1,0:T(8,128)(2,1)}, bf16[4,64,2048]{2,1,0:T(8,128)(2,1)}, bf16[4,64,2048]{2,1,0:T(8,128)(2,1)}, bf16[256,2048]{1,0:T(8,128)(2,1)}...) custom-call(bf16[32,2048]{1,0:T(8,128)(2,1)} %x_ref.1, bf16[32,2048]{1,0:T(8,128)(2,1)} %g_ref.1, ...), custom_call_target="tpu_custom_call" | custom-call | flops 10737418240 | bytes 25165824 | tf_op jit(solution)/shard_map/pallas_call | solution.py:311
  95.2 0.0 copy-start
  95.3 0.0 copy-start.3
  95.3 7.5 %convolution_convert_fusion.1 = bf16[2048,2048]{1,0:T(8,128)(2,1)} fusion(bf16[256,2048]{1,0:T(8,128)(2,1)} %bitcast.8, bf16[256,2048]{1,0:T(8,128)(2,1)} %get-tuple-element.13), kind=kOutput, calls=%fused_computation.1 | convolution fusion | flops 2151677952 | bytes 10485760 | tf_op jit(solution)/shard_map/dot_general | solution.py:355
  102.7 0.0 copy-done
  102.7 0.0 copy-done.3
  102.7 0.0 copy-start.1
  102.7 0.0 copy-start.2
  102.8 5.8 %convolution_convert_fusion.2 = bf16[2048,2048]{1,0:T(8,128)(2,1)} fusion(bf16[256,2048]{1,0:T(8,128)(2,1)S(1)} %bitcast.9, bf16[256,2048]{1,0:T(8,128)(2,1)S(1)} %copy-done.3), kind=kOutput, calls=%fused_computation.2 | convolution fusion | flops 2151677952 | bytes 10485760 | tf_op jit(solution)/shard_map/dot_general | solution.py:355
  108.5 0.0 copy-done.1
  108.5 0.0 copy-done.2
  108.5 0.0 copy-start.4
  108.5 5.8 %convolution_convert_fusion = bf16[2048,2048]{1,0:T(8,128)(2,1)} fusion(bf16[256,2048]{1,0:T(8,128)(2,1)S(1)} %copy-done.1, bf16[256,2048]{1,0:T(8,128)(2,1)S(1)} %bitcast.10), kind=kOutput, calls=%fused_computation | convolution fusion | flops 2151677952 | bytes 10485760 | tf_op jit(solution)/shard_map/dot_general | solution.py:355
  114.3 0.0 copy-done.4
  114.3 0.7 copy.10
Async XLA Ops:
  95.2 7.5 %copy-start = (bf16[4,64,2048]{2,1,0:T(8,128)(2,1)S(1)}, bf16[4,64,2048]{2,1,0:T(8,128)(2,1)}, u32[]{:S(2)}) copy-start(bf16[4,64,2048]{2,1,0:T(8,128)(2,1)} %get-tuple-element.11) | copy-start | bytes 3145732
  95.3 7.5 %copy-start.3 = (bf16[256,2048]{1,0:T(8,128)(2,1)S(1)}, bf16[256,2048]{1,0:T(8,128)(2,1)}, u32[]{:S(2)}) copy-start(bf16[256,2048]{1,0:T(8,128)(2,1)} %get-tuple-element.12) | copy-start | bytes 3145732
  102.7 5.8 %copy-start.1 = (bf16[256,2048]{1,0:T(8,128)(2,1)S(1)}, bf16[256,2048]{1,0:T(8,128)(2,1)}, u32[]{:S(2)}) copy-start(bf16[256,2048]{1,0:T(8,128)(2,1)} %get-tuple-element.14) | copy-start | bytes 3145732
  102.7 5.8 %copy-start.2 = (bf16[4,64,2048]{2,1,0:T(8,128)(2,1)S(1)}, bf16[4,64,2048]{2,1,0:T(8,128)(2,1)}, u32[]{:S(2)}) copy-start(bf16[4,64,2048]{2,1,0:T(8,128)(2,1)} %get-tuple-element.15) | copy-start | bytes 3145732
  108.5 5.8 %copy-start.4 = (bf16[32,2048]{1,0:T(8,128)(2,1)S(1)}, bf16[32,2048]{1,0:T(8,128)(2,1)}, u32[]{:S(2)}) copy-start(bf16[32,2048]{1,0:T(8,128)(2,1)} %get-tuple-element.20) | copy-start | bytes 393220

commit v3 on v2

--- a/solution.py
+++ b/solution.py
@@ -11,6 +11,7 @@
 BF16, F32 = jnp.bfloat16, jnp.float32
 REST = (((1,), (1,)), ((), ()))
 LAG = 2
+TILE = 256
 
 
 def remote(src, dst, send, recv, device):
@@ -292,6 +293,53 @@
         pair(k).wait_send()
     for k in range(1, chips):
         across(k).wait_send()
+
+
+def products(x_ref, h_ref, g_ref, gd_ref, ud_ref, wg_ref, wu_ref, wd_ref):
+    contract = (((0,), (0,)), ((), ()))
+    for left, right, out in ((x_ref, gd_ref, wg_ref), (x_ref, ud_ref, wu_ref), (h_ref, g_ref, wd_ref)):
+        width = out.shape[1]
+        piece = min(512, width)
+        for p in range(width // piece):
+            cols = slice(p * piece, (p + 1) * piece)
+            out[:, cols] = lax.dot_general(
+                left[...], right[:, cols], contract, preferred_element_type=F32
+            ).astype(BF16)
+
+
+def weight_grads(x_all, g_all, hidden, gate_delta, up_delta):
+    rows, dl = x_all.shape
+    fl = hidden.shape[1]
+    tiles = max(1, min(dl, fl) // TILE)
+    dt, ft = dl // tiles, fl // tiles
+    whole = lambda i: (0, 0)
+    column = lambda i: (0, i)
+    band = lambda i: (i, 0)
+    return pl.pallas_call(
+        products,
+        grid=(tiles,),
+        out_shape=(
+            jax.ShapeDtypeStruct((dl, fl), BF16),
+            jax.ShapeDtypeStruct((dl, fl), BF16),
+            jax.ShapeDtypeStruct((fl, dl), BF16),
+        ),
+        in_specs=[
+            pl.BlockSpec((rows, dt), column),
+            pl.BlockSpec((rows, ft), column),
+            pl.BlockSpec((rows, dl), whole),
+            pl.BlockSpec((rows, fl), whole),
+            pl.BlockSpec((rows, fl), whole),
+        ],
+        out_specs=(
+            pl.BlockSpec((dt, fl), band),
+            pl.BlockSpec((dt, fl), band),
+            pl.BlockSpec((ft, dl), band),
+        ),
+        compiler_params=pltpu.CompilerParams(vmem_limit_bytes=60 * 2**20),
+        cost_estimate=pl.CostEstimate(
+            flops=6 * rows * dl * fl, bytes_accessed=6 * dl * fl + 10 * rows * dl, transcendentals=0
+        ),
+    )(x_all, hidden, g_all, gate_delta, up_delta)
 
 
 def on_device(nr, nc, x, g, wg, wu, wd):
@@ -349,12 +397,7 @@
         cost_estimate=pl.CostEstimate(flops=flops, bytes_accessed=6 * dl * fl, transcendentals=rows * fl),
     )(x, g, wg, wu, wd)
     x_all, g_all = x_all.reshape(rows, dl), g_all.reshape(rows, dl)
-    contract = (((0,), (0,)), ((), ()))
-
-    def wgrad(a, b):
-        return lax.dot_general(a, b, contract, preferred_element_type=F32).astype(BF16)
-
-    return grad, wgrad(x_all, gate_delta), wgrad(x_all, up_delta), wgrad(hidden, g_all)
+    return (grad, *weight_grads(x_all, g_all, hidden, gate_delta, up_delta))
 
 
 def solution(mesh):

time: 115 us -> 108 us (0.939)
  matrix products: 19 us -> 0 us
  Pallas kernels: 94.6 us -> 107 us
    dot_general x3 -> x0, matrix products: 19 us -> none  [wgrad(): lax.dot_general(a, b, contract, preferred_element_type=F32).astype(BF16)]
    pallas_call x0 -> x1, Pallas kernels: none -> 12.2 us  [weight_grads(): pl.pallas_call(products, grid=(tiles,), out_shape=(jax.ShapeDtypeStruct((...]
where the time goes in v3:
time: 108 us
  Pallas kernels  107 us (99%)
    pallas_call x1, Pallas kernels, on_device(): pl.pallas_call(functools.partial(kernel, nr, nc, fc), out_shape=(jax.Shap...  94.6 us
    pallas_call x1, Pallas kernels, weight_grads(): pl.pallas_call(products, grid=(tiles,), out_shape=(jax.ShapeDtypeStruct((...  12.2 us

profile of v3, /device:TPU:0, one launch (start us, length us, event | category | flops | bytes accessed | tf_op | source)
XLA Modules:
  0.0 108.1 jit_solution(7826478616872503651)
XLA Ops:
  0.6 94.6 %shard_map.84 = (bf16[32,2048]{1,0:T(8,128)(2,1)}, bf16[4,64,2048]{2,1,0:T(8,128)(2,1)}, bf16[4,64,2048]{2,1,0:T(8,128)(2,1)}, bf16[256,2048]{1,0:T(8,128)(2,1)}...) custom-call(bf16[32,2048]{1,0:T(8,128)(2,1)} %x_ref.1, bf16[32,2048]{1,0:T(8,128)(2,1)} %g_ref.1, ...), custom_call_target="tpu_custom_call" | custom-call | flops 10737418240 | bytes 25165824 | tf_op jit(solution)/shard_map/pallas_call | solution.py:359
  95.2 0.0 copy-start
  95.3 12.2 %shard_map.85 = (bf16[2048,2048]{1,0:T(8,128)(2,1)}, bf16[2048,2048]{1,0:T(8,128)(2,1)}, bf16[2048,2048]{1,0:T(8,128)(2,1)}) custom-call(bf16[256,2048]{1,0:T(8,128)(2,1)} %bitcast.2, bf16[256,2048]{1,0:T(8,128)(2,1)} %get-tuple-element.15.h_ref, bf16[256,2048]{1,0:T(8,128)(2,1)} %bitcast.3, bf16[256,2048]{1,0:T(8,128)(2,1)} %get-tuple-element.17.gd_ref, ...), custom_call_target="tpu_custom_call" | custom-call | flops 6442450944 | bytes 30408704 | tf_op jit(solution)/shard_map/pallas_call | solution.py:318
  107.4 0.0 copy-done
  107.4 0.7 copy.10
Async XLA Ops:
  95.2 12.2 %copy-start = (bf16[32,2048]{1,0:T(8,128)(2,1)S(1)}, bf16[32,2048]{1,0:T(8,128)(2,1)}, u32[]{:S(2)}) copy-start(bf16[32,2048]{1,0:T(8,128)(2,1)} %get-tuple-element.26) | copy-start | bytes 393220
